TPU v7x, 512 devices: a whole 4x4x16 slice. The times are simulated.
512 devices in a mesh: dp: 64 (over y, z), mp: 8 (over x, core).
Axes of the slice: x: 4, y: 4, z: 16, core: 2. Of those that a mesh axis runs over, the one named last changes fastest.
Arguments:
- gradient: bfloat16 [8, 64, 512, 512], P('mp', None, 'dp'), may hold values from -80 to 80
- left_root: bfloat16 [8, 64, 512, 512], P('mp', 'dp'), may hold values from -1 to 4
- right_root: bfloat16 [8, 64, 512, 512], P('mp', 'dp'), may hold values from -1 to 4
- slot_table: int32 [8, 64], P('mp'), may hold values from 0 to 63, each once within a row
- overflow: int32 [8, 64, 64], P('mp', None, 'dp'), may hold values 0 or 1
Outputs:
- update: bfloat16 [8, 64, 512, 512], P('mp', None, 'dp')
Inputs may be any that keep to these rules, and one draw needn't show every extreme that they name: `slot_table`: each row names every slot 0 to 63 once; slot s of group g is held by the device of index s along dp.
All inputs are finite; a program needn't handle non-finite values. No bound on the sum of `overflow` on one device may be relied on, other than what follows from the above.
Results may differ from a plain program's by a relative error of at most 0.0049.
Values may be sent and summed in bfloat16 or wider, within the bound.
No kernel may reach another device: no remote copies, remote signals or barrier semaphores. Data moves between devices by JAX's collectives and lax.ppermute only.
A program may use at most 64 MiB of HBM per device.

v0:
```python
import math

import jax
import jax.numpy as jnp
from jax import lax
from jax.sharding import PartitionSpec as P

BS = 512


def on_device(gradient, left_root, right_root, slot_table, overflow):
    slot_count = gradient.shape[1]
    slot_of = slot_table[0]
    block_at = (
        jnp.zeros((slot_count,), jnp.int32).at[slot_of].set(jnp.arange(slot_count, dtype=jnp.int32))
    )
    row_tiles = gradient[0][block_at]
    flag_rows = overflow[0][block_at]
    blocks, flag_grid = (
        lax.all_to_all(row_tiles, "dp", split_axis=0, concat_axis=1, tiled=True),
        lax.all_to_all(flag_rows, "dp", split_axis=0, concat_axis=1, tiled=True),
    )
    keep_mask = (jnp.max(flag_grid, axis=1) == 0).astype(jnp.float32)
    block_sq = jnp.sum(jnp.square(blocks.astype(jnp.float32)), axis=(1, 2))
    local_term = jnp.sum(block_sq * keep_mask)
    grand_total = lax.psum(local_term, ("dp", "mp"))
    blocks_all = slot_count * lax.axis_size("mp")
    clip_factor = jnp.minimum(
        jnp.float32(1.0), BS * math.sqrt(blocks_all) / jnp.sqrt(grand_total + 1e-06)
    )
    left_product = jnp.dot(left_root[0, 0], blocks[0], preferred_element_type=jnp.float32).astype(
        jnp.bfloat16
    )
    preconditioned = jnp.dot(left_product, right_root[0, 0], preferred_element_type=jnp.float32)
    pre_sq = jnp.sum(preconditioned * preconditioned)
    scaled = (
        preconditioned
        * (jnp.sqrt(block_sq[0]) / jnp.sqrt(pre_sq + 1e-06))
        * keep_mask[0]
        * clip_factor
    )
    updates = [scaled.astype(jnp.bfloat16)]
    stacked = jnp.stack(updates)
    returned = lax.all_to_all(stacked, "dp", split_axis=1, concat_axis=0, tiled=True)
    result = returned[slot_of]
    return result[None]


def solution(mesh):
    return jax.shard_map(
        on_device,
        mesh=mesh,
        in_specs=(
            P("mp", None, "dp", None),
            P("mp", "dp", None, None),
            P("mp", "dp", None, None),
            P("mp", None),
            P("mp", None, "dp"),
        ),
        out_specs=P("mp", None, "dp", None),
        check_vma=False,
    )
```

profile of v0, /device:TPU:6, one launch (start us, length us, event | category | flops | bytes accessed | tf_op | source)
XLA Modules:
  0.0 224.1 jit_solution(8304646061729853946)
XLA Ops:
  0.0 0.0 copy-start
  0.0 0.7 fusion.7
  0.7 0.8 scatter_custom_fusion
  1.5 0.0 copy-start.1
  1.5 0.6 copy-done.1
  2.2 0.8 gather_fusion.1
  3.0 0.7 copy.8
  3.7 18.7 %all-to-all-start.1 = ((s32[64,1,1]{2,1,0:T(1,128)}), s32[64,1,1]{2,1,0:T(1,128)S(1)}, u32[]{:S(2)}, u32[]{:S(2)}) async-start(s32[64,1,1]{2,1,0:T(1,128)} %copy.8), calls=%async_computation.1 | async-start | bytes 65536 | tf_op jit(solution)/shard_map/all_to_all | solution.py:21
  22.4 0.0 copy-done
  22.4 1.4 gather_fusion
  23.8 12.9 %all-to-all-done.1 = s32[64,1,1]{2,1,0:T(1,128)S(1)} async-done(((s32[64,1,1]{2,1,0:T(1,128)}), s32[64,1,1]{2,1,0:T(1,128)S(1)}, u32[]{:S(2)}, u32[]{:S(2)}) %all-to-all-start.1) | async-done | bytes 288 | tf_op jit(solution)/shard_map/all_to_all | solution.py:21
  36.7 0.0 copy-start.3
  36.7 4.8 %all-to-all-start = ((bf16[64,8,512]{2,1,0:T(8,128)(2,1)}), bf16[64,8,512]{2,1,0:T(8,128)(2,1)S(1)}, u32[]{:S(2)}, u32[]{:S(2)}) async-start(bf16[64,8,512]{2,1,0:T(8,128)(2,1)} %gather_fusion), calls=%async_computation | async-start | bytes 1048576 | tf_op jit(solution)/shard_map/all_to_all | solution.py:20
  41.4 0.0 copy-start.2
  41.5 0.8 reduce_max.9
  42.9 29.3 %all-to-all-done = bf16[64,8,512]{2,1,0:T(8,128)(2,1)S(1)} async-done(((bf16[64,8,512]{2,1,0:T(8,128)(2,1)}), bf16[64,8,512]{2,1,0:T(8,128)(2,1)S(1)}, u32[]{:S(2)}, u32[]{:S(2)}) %all-to-all-start) | async-done | bytes 524320 | tf_op jit(solution)/shard_map/all_to_all | solution.py:20
  72.3 0.9 multiply_reduce_fusion.1
  74.5 0.0 copy-done.3
  74.5 0.0 copy-done.2
  74.5 1.6 multiply_reduce_fusion
  76.8 99.3 %psum.7 = f32[]{:T(128)} all-reduce(f32[]{:T(128)S(6)} %mul.29), channel_id=1, replica_groups=mesh['dp'=64,'mp'=8] {'dp','mp'}, use_global_device_ids=true, to_apply=%region_4.0 | all-reduce | flops 1 | bytes 8 | tf_op jit(solution)/shard_map/psum | solution.py:26
  176.8 0.1 fusion.1
  176.9 0.8 copy.14
  177.8 0.5 broadcast.46
  178.3 3.8 %reduce.4 = bf16[512,512]{1,0:T(8,128)(2,1)S(1)} reduce(bf16[512,1,512]{2,1,0:T(2,128)(2,1)S(1)} %bitcast.37, bf16[]{:T(256)} %broadcast.46), dimensions={1}, to_apply=%bitcast.33.reduce_sub_computation | reduce | bytes 1048578
  182.1 1.0 reshape.97
  183.1 7.3 %all-to-all-start.2 = ((bf16[64,2,2048]{2,1,0:T(2,128)(2,1)}), bf16[64,2,2048]{2,1,0:T(2,128)(2,1)S(1)}, u32[]{:S(2)}, u32[]{:S(2)}) async-start(bf16[64,2,2048]{2,1,0:T(2,128)(2,1)} %reshape.97), calls=%async_computation.2 | async-start | bytes 1048576 | tf_op jit(solution)/shard_map/all_to_all | solution.py:44
  190.4 31.7 %all-to-all-done.2 = bf16[64,2,2048]{2,1,0:T(2,128)(2,1)S(1)} async-done(((bf16[64,2,2048]{2,1,0:T(2,128)(2,1)}), bf16[64,2,2048]{2,1,0:T(2,128)(2,1)S(1)}, u32[]{:S(2)}, u32[]{:S(2)}) %all-to-all-start.2) | async-done | bytes 524320 | tf_op jit(solution)/shard_map/all_to_all | solution.py:44
  222.1 0.5 reshape.98
  222.6 0.1 copy.13
  222.7 1.4 gather_fusion.2
  (4 shorter events, 0.0 us)
Async XLA Ops:
  0.0 22.4 %copy-start = (bf16[1,64,8,512]{3,2,1,0:T(8,128)(2,1)S(1)}, bf16[1,64,8,512]{3,2,1,0:T(8,128)(2,1)}, u32[]{:S(2)}) copy-start(bf16[1,64,8,512]{3,2,1,0:T(8,128)(2,1)} %param.5) | copy-start | bytes 1572868
  1.5 0.7 copy-start.1
  3.7 33.0 %all-to-all-start.1 = ((s32[64,1,1]{2,1,0:T(1,128)}), s32[64,1,1]{2,1,0:T(1,128)S(1)}, u32[]{:S(2)}, u32[]{:S(2)}) async-start(s32[64,1,1]{2,1,0:T(1,128)} %copy.8), calls=%async_computation.1 | async-start | bytes 65536 | tf_op jit(solution)/shard_map/all_to_all | solution.py:21
  36.7 37.8 %copy-start.3 = (bf16[1,1,512,512]{3,2,1,0:T(8,128)(2,1)S(1)}, bf16[1,1,512,512]{3,2,1,0:T(8,128)(2,1)}, u32[]{:S(2)}) copy-start(bf16[1,1,512,512]{3,2,1,0:T(8,128)(2,1)} %param.6) | copy-start | bytes 1572868
  36.7 35.6 %all-to-all-start = ((bf16[64,8,512]{2,1,0:T(8,128)(2,1)}), bf16[64,8,512]{2,1,0:T(8,128)(2,1)S(1)}, u32[]{:S(2)}, u32[]{:S(2)}) async-start(bf16[64,8,512]{2,1,0:T(8,128)(2,1)} %gather_fusion), calls=%async_computation | async-start | bytes 1048576 | tf_op jit(solution)/shard_map/all_to_all | solution.py:20
  41.4 33.0 %copy-start.2 = (bf16[1,1,512,512]{3,2,1,0:T(8,128)(2,1)S(1)}, bf16[1,1,512,512]{3,2,1,0:T(8,128)(2,1)}, u32[]{:S(2)}) copy-start(bf16[1,1,512,512]{3,2,1,0:T(8,128)(2,1)} %param.7) | copy-start | bytes 1572868
  183.1 39.0 %all-to-all-start.2 = ((bf16[64,2,2048]{2,1,0:T(2,128)(2,1)}), bf16[64,2,2048]{2,1,0:T(2,128)(2,1)S(1)}, u32[]{:S(2)}, u32[]{:S(2)}) async-start(bf16[64,2,2048]{2,1,0:T(2,128)(2,1)} %reshape.97), calls=%async_computation.2 | async-start | bytes 1048576 | tf_op jit(solution)/shard_map/all_to_all | solution.py:44
where the time goes:
time: 227 us; the launch traced here: 224 us
  blocking collectives  99.3 us (44%)
  waiting for transfers between devices  73.9 us (33%)
  starting transfers between devices  30.8 us (14%)
  local copies, waits for them, and re-layouts  8.65 us (4%)
  other arithmetic  6.34 us (3%)
  between operations  3.57 us (2%)
    psum x1, blocking collectives, on_device(): grand_total = lax.psum(local_term, ('dp', 'mp'))  99.3 us
    all_to_all x1, waiting for transfers between devices, on_device(): lax.all_to_all(stacked, 'dp', split_axis=1, concat_axis=0, tiled=True)  31.7 us
    all_to_all x1, waiting for transfers between devices, on_device(): lax.all_to_all(row_tiles, 'dp', split_axis=0, concat_axis=1, tiled=True)  29.3 us
    all_to_all x1, starting transfers between devices, on_device(): lax.all_to_all(flag_rows, 'dp', split_axis=0, concat_axis=1, tiled=True)  18.7 us
    all_to_all x1, waiting for transfers between devices, on_device(): lax.all_to_all(flag_rows, 'dp', split_axis=0, concat_axis=1, tiled=True)  12.9 us
    all_to_all x1, starting transfers between devices, on_device(): lax.all_to_all(stacked, 'dp', split_axis=1, concat_axis=0, tiled=True)  7.26 us
    all_to_all x1, starting transfers between devices, on_device(): lax.all_to_all(row_tiles, 'dp', split_axis=0, concat_axis=1, tiled=True)  4.77 us
  transfers between devices with their start and end apart: 3, of which 3 were waited for; matrix products, arithmetic and copies ran while one was open for 1% of the time, Pallas kernels for 0%

commit v1 on v0

v1 whole, which is shorter than its diff:
```python
import functools
import math

import jax
import jax.numpy as jnp
from jax import lax
from jax.experimental import pallas as pl
from jax.experimental.pallas import tpu as pltpu
from jax.sharding import PartitionSpec as P

MARK = 1e30
LIMIT = 1e29

LANES = 128
PART = 4
PIECES = 4

SMEM = pl.BlockSpec(memory_space=pltpu.SMEM)
VMEM = pl.BlockSpec(memory_space=pltpu.VMEM)
HBM = pl.BlockSpec(memory_space=pltpu.HBM)
AFTER_PARAMS = pltpu.CompilerParams(vmem_limit_bytes=63_200_000)
PARAMS = pltpu.CompilerParams(vmem_limit_bytes=32 * 1024 * 1024)


def sum_squares(flag_ref, grad_ref, partial_ref, lanes_ref):
    cols = grad_ref.shape[2]
    for b in range(lanes_ref.shape[0]):
        wide = grad_ref[b].astype(jnp.float32)
        square = wide * wide
        lane = square[:, 0:LANES]
        for c in range(LANES, cols, LANES):
            lane = lane + square[:, c : c + LANES]
        lane = jnp.sum(lane, axis=0, keepdims=True)
        flagged = flag_ref[0, b] != 0
        lanes_ref[b : b + 1, :] = jnp.where(flagged, jnp.full_like(lane, MARK), lane)
    partial_ref[...] = jnp.sum(lanes_ref[...].T, axis=0, keepdims=True)


def send_kernel(
    slot_hbm,
    flag_hbm,
    grad_hbm,
    rows_hbm,
    partial_hbm,
    slot_ref,
    flag_ref,
    tiles_ref,
    part_ref,
    lanes_ref,
    loads,
    sem,
):
    slots = rows_hbm.shape[0]
    tables = [
        pltpu.make_async_copy(slot_hbm, slot_ref, loads.at[PIECES]),
        pltpu.make_async_copy(flag_hbm, flag_ref, loads.at[PIECES + 1]),
    ]
    for copy in tables:
        copy.start()
    pieces = []
    for piece in range(PIECES):
        span = pl.ds(piece * slots // PIECES, slots // PIECES)
        pieces.append(
            pltpu.make_async_copy(grad_hbm.at[span], tiles_ref.at[span], loads.at[piece])
        )
        pieces[-1].start()
    tiles_ref[slots] = jnp.full(tiles_ref.shape[1:], jnp.inf, tiles_ref.dtype)
    for copy in tables:
        copy.wait()
    for piece in range(PIECES):
        pieces[piece].wait()
        for b in range(piece * slots // PIECES, (piece + 1) * slots // PIECES):
            flagged = flag_ref[0, b] != 0
            source = jnp.where(flagged, slots, b)
            pltpu.make_async_copy(
                tiles_ref.at[source], rows_hbm.at[slot_ref[0, b]], sem
            ).start()

    sum_squares(flag_ref, tiles_ref, part_ref, lanes_ref)
    part_copy = pltpu.make_async_copy(part_ref, partial_hbm, loads.at[PIECES])
    part_copy.start()
    pltpu.make_async_copy(tiles_ref.at[pl.ds(0, slots)], rows_hbm, sem).wait()
    part_copy.wait()


def after_kernel(rows_ref, swapped_ref, out_ref):
    del rows_ref, swapped_ref, out_ref


def block_kernel(block_ref, left_ref, right_ref, sums_ref, out_ref):
    slots, places = out_ref.shape[0:2]
    order, cols = block_ref.shape
    parts = order // (slots * PART)
    block = block_ref[...]
    wide = block.astype(jnp.float32)
    block_sq = jnp.sum(wide * wide, keepdims=True)
    keep = block_sq < LIMIT
    left_product = jnp.dot(left_ref[...], block, preferred_element_type=jnp.float32).astype(
        jnp.bfloat16
    )
    preconditioned = jnp.dot(left_product, right_ref[...], preferred_element_type=jnp.float32)
    pre_sq = jnp.sum(preconditioned * preconditioned, keepdims=True)
    ratio = jnp.sqrt(block_sq) / jnp.sqrt(pre_sq + 1e-06)
    scaled = jnp.where(keep, preconditioned * ratio, 0.0)
    for c in range(0, cols, LANES):
        tiles = scaled[:, c : c + LANES].reshape(slots, parts, PART, LANES).astype(jnp.bfloat16)
        place = c // LANES * parts
        out_ref[:, place : place + parts] = tiles
    sums = sums_ref[...].astype(jnp.bfloat16)
    both = jnp.concatenate([sums[0:PART], sums[PART : 2 * PART]], axis=1)
    for s in range(slots):
        out_ref[s, places - 1] = both


def finish_kernel(bound, slot_table_ref, rows_ref, out_hbm, slot_ref, out_ref, sems):
    slots, rows, cols = out_ref.shape
    table = pltpu.make_async_copy(slot_table_ref, slot_ref, sems.at[PIECES])
    table.start()
    parts = rows // PART
    owed = rows_ref[:, rows_ref.shape[1] - 1].astype(jnp.float32)
    squares = jnp.sum(owed, axis=0)
    grand_total = jnp.sum(jnp.where(squares < LIMIT, squares, 0.0), keepdims=True)
    clip = jnp.minimum(1.0, bound / jnp.sqrt(grand_total + 1e-06))
    table.wait()
    copies = []
    for piece in range(PIECES):
        first, last = piece * slots // PIECES, (piece + 1) * slots // PIECES
        for b in range(first, last):
            slot = slot_ref[0, b]
            for c in range(0, cols, LANES):
                place = c // LANES * parts
                tile = rows_ref[slot, place : place + parts].astype(jnp.float32)
                out_ref[b, :, c : c + LANES] = (tile.reshape(rows, LANES) * clip).astype(
                    jnp.bfloat16
                )
        span = pl.ds(first, last - first)
        copy = pltpu.make_async_copy(out_ref.at[span], out_hbm.at[span], sems.at[piece])
        copy.start()
        copies.append(copy)
    for copy in copies:
        copy.wait()


def swapped(value, size, core, step):
    return lax.ppermute(value, "mp", [(i, i ^ step) for i in range(core, size, 2)])


def on_device(n_mp, gradient, left_root, right_root, slot_table, overflow):
    slots, rows, cols = gradient.shape[1:]
    order = left_root.shape[-1]
    flags = overflow.reshape(1, slots)
    row_tiles, partial = pl.pallas_call(
        send_kernel,
        out_shape=(
            jax.ShapeDtypeStruct((slots, rows, cols), jnp.bfloat16),
            jax.ShapeDtypeStruct((1, slots), jnp.float32),
        ),
        in_specs=[HBM] * 3,
        out_specs=(HBM, HBM),
        scratch_shapes=[
            pltpu.SMEM((1, slots), jnp.int32),
            pltpu.SMEM((1, slots), jnp.int32),
            pltpu.VMEM((slots + 1, rows, cols), jnp.bfloat16),
            pltpu.VMEM((1, slots), jnp.float32),
            pltpu.VMEM((slots, LANES), jnp.float32),
            pltpu.SemaphoreType.DMA((PIECES + 2,)),
            pltpu.SemaphoreType.DMA,
        ],
        name="send",
    )(slot_table, flags, gradient[0])

    first = swapped(partial, n_mp, 0, 2)
    second = swapped(jnp.concatenate([partial, first], axis=0), n_mp, 0, 4)
    row_tiles = pl.pallas_call(
        after_kernel,
        out_shape=jax.ShapeDtypeStruct(row_tiles.shape, row_tiles.dtype),
        in_specs=[HBM, pl.BlockSpec(memory_space=pl.ANY)],
        out_specs=HBM,
        input_output_aliases={0: 0},
        compiler_params=AFTER_PARAMS,
        name="after",
    )(row_tiles, second)
    blocks = lax.all_to_all(row_tiles, "dp", split_axis=0, concat_axis=0, tiled=True)
    again = partial + second[0:1]
    first_1 = swapped(again, n_mp, 1, 2)
    second_1 = swapped(jnp.concatenate([again, first_1], axis=0), n_mp, 1, 4)
    own = jnp.concatenate([partial, first + first_1, second + second_1], axis=0)
    other = lax.ppermute(own, "mp", [(i, i ^ 1) for i in range(n_mp)])
    sums = jnp.concatenate([own, other], axis=0)

    places = order * cols // (slots * PART * LANES) + 1
    scaled = pl.pallas_call(
        block_kernel,
        out_shape=jax.ShapeDtypeStruct((slots, places, PART, LANES), jnp.bfloat16),
        in_specs=[VMEM] * 4,
        out_specs=VMEM,
        compiler_params=PARAMS,
        name="block",
    )(blocks.reshape(order, cols), left_root[0, 0], right_root[0, 0], sums)

    returned = lax.all_to_all(scaled, "dp", split_axis=0, concat_axis=0, tiled=True)
    result = pl.pallas_call(
        functools.partial(finish_kernel, order * math.sqrt(slots * n_mp)),
        out_shape=jax.ShapeDtypeStruct((slots, rows, cols), jnp.bfloat16),
        in_specs=[VMEM, VMEM],
        out_specs=HBM,
        scratch_shapes=[
            pltpu.SMEM((1, slots), jnp.int32),
            pltpu.VMEM((slots, rows, cols), jnp.bfloat16),
            pltpu.SemaphoreType.DMA((PIECES + 1,)),
        ],
        compiler_params=PARAMS,
        name="finish",
    )(slot_table, returned)
    return result[None]


def solution(mesh):
    return jax.shard_map(
        functools.partial(on_device, mesh.shape["mp"]),
        mesh=mesh,
        in_specs=(
            P("mp", None, "dp", None),
            P("mp", "dp", None, None),
            P("mp", "dp", None, None),
            P("mp", None),
            P("mp", None, "dp"),
        ),
        out_specs=P("mp", None, "dp", None),
        check_vma=False,
    )
```

time: 227 us -> 92.1 us (0.41); the launches traced: 224 us -> 91.8 us
  blocking collectives: 99.3 us -> 32.7 us
  waiting for transfers between devices: 73.9 us -> 22 us
  local copies, waits for them, and re-layouts: 8.65 us -> 1.15 us
  other arithmetic: 6.34 us -> 0.68 us
  Pallas kernels: 0 us -> 4.77 us
  between operations: 3.57 us -> 0.15 us
    psum x1 -> x0, blocking collectives: 99.3 us -> none  [on_device(): grand_total = lax.psum(local_term, ('dp', 'mp'))]
    all_to_all x3 -> x1, waiting for transfers between devices: 73.9 us -> 16.7 us  [on_device(): lax.all_to_all(row_tiles, 'dp', split_axis=0, concat_axis=0, tiled=True)]
    all_to_all x0 -> x1, blocking collectives: none -> 32.7 us  [on_device(): lax.all_to_all(scaled, 'dp', split_axis=0, concat_axis=0, tiled=True)]
    all_to_all x3 -> x1, starting transfers between devices: 30.8 us -> 17.1 us  [on_device(): lax.all_to_all(row_tiles, 'dp', split_axis=0, concat_axis=0, tiled=True)]
    ppermute x0 -> x5, starting transfers between devices: none -> 13.2 us  [the longest x4 11.2 us: swapped(): lax.ppermute(value, 'mp', [(i, i ^ step) for i in range(core, size, 2)])]
    ppermute x0 -> x5, waiting for transfers between devices: none -> 5.35 us  [the longest x4 4.23 us: swapped(): lax.ppermute(value, 'mp', [(i, i ^ step) for i in range(core, size, 2)])]
    pallas_call x0 -> x4, Pallas kernels: none -> 4.77 us  [the longest x1 1.98 us: on_device(): pl.pallas_call(send_kernel, out_shape=(jax.ShapeDtypeStruct((slots, rows,...]
    unnamed x1 -> x0, other arithmetic: 3.82 us -> none
  transfers between devices with their start and end apart: 3 -> 6, of which waited for: 3 -> 4; matrix products, arithmetic and copies ran while one was open for 1% -> 1% of each run, Pallas kernels for 0% -> 0%
where the time goes in v1:
time: 92.1 us; the launch traced here: 91.8 us
  blocking collectives  32.7 us (36%)
  starting transfers between devices  30.2 us (33%)
  waiting for transfers between devices  22 us (24%)
  Pallas kernels  4.77 us (5%)
  local copies, waits for them, and re-layouts  1.15 us (1%)
    all_to_all x1, blocking collectives, on_device(): lax.all_to_all(scaled, 'dp', split_axis=0, concat_axis=0, tiled=True)  32.7 us
    all_to_all x1, starting transfers between devices, on_device(): lax.all_to_all(row_tiles, 'dp', split_axis=0, concat_axis=0, tiled=True)  17.1 us
    all_to_all x1, waiting for transfers between devices, on_device(): lax.all_to_all(row_tiles, 'dp', split_axis=0, concat_axis=0, tiled=True)  16.7 us
    ppermute x4, starting transfers between devices, swapped(): lax.ppermute(value, 'mp', [(i, i ^ step) for i in range(core, size, 2)])  11.2 us
    ppermute x4, waiting for transfers between devices, swapped(): lax.ppermute(value, 'mp', [(i, i ^ step) for i in range(core, size, 2)])  4.23 us
    pallas_call x1, Pallas kernels, on_device(): pl.pallas_call(send_kernel, out_shape=(jax.ShapeDtypeStruct((slots, rows,...  1.98 us
    ppermute x1, starting transfers between devices, on_device(): other = lax.ppermute(own, 'mp', [(i, i ^ 1) for i in range(n_mp)])  1.92 us
  transfers between devices with their start and end apart: 6, of which 4 were waited for; matrix products, arithmetic and copies ran while one was open for 1% of the time, Pallas kernels for 0%

profile of v1, /device:TPU:6, one launch (start us, length us, event | category | flops | bytes accessed | tf_op | source)
XLA Modules:
  0.0 91.8 jit_solution(6462243279811348753)
XLA Ops:
  0.0 2.0 %send.1 = (bf16[64,8,512]{2,1,0:T(8,128)(2,1)}, f32[1,64]{1,0:T(1,128)}) custom-call(s32[1,64]{1,0:T(1,128)} %slot_table_ref.1, s32[1,64]{1,0:T(1,128)} %bitcast.10, bf16[64,8,512]{2,1,0:T(8,128)(2,1)} %bitcast.9), custom_call_target="tpu_custom_call" | custom-call | tf_op jit(solution)/shard_map/send/pallas_call | solution.py:152
  2.0 0.0 copy-start.3
  2.0 0.6 copy-done.3
  2.6 2.7 %collective-permute-start = (f32[1,64]{1,0:T(1,128)S(1)}, f32[1,64]{1,0:T(1,128)S(1)}, u32[]{:S(2)}, u32[]{:S(2)}) collective-permute-start(f32[1,64]{1,0:T(1,128)S(1)} %copy-done.3), channel_id=1, source_target_pairs={{0,2},{2,0},{4,6},{6,4},{8,10},{10,8},{12,14},{14,12},{16,18},{18,... | collective-permute-start | bytes 776 | tf_op jit(solution)/shard_map/ppermute | solution.py:145
  5.3 2.7 %collective-permute-done = f32[1,64]{1,0:T(1,128)S(1)} collective-permute-done((f32[1,64]{1,0:T(1,128)S(1)}, f32[1,64]{1,0:T(1,128)S(1)}, u32[]{:S(2)}, u32[]{:S(2)}) %collective-permute-start) | collective-permute-done | bytes 288 | tf_op jit(solution)/shard_map/ppermute | solution.py:145
  8.0 7.2 %collective-permute-start.1 = (f32[2,64]{1,0:T(2,128)S(1)}, f32[2,64]{1,0:T(2,128)S(1)}, u32[]{:S(2)}, u32[]{:S(2)}) collective-permute-start(f32[2,64]{1,0:T(2,128)S(1)} %pad_maximum_fusion.2), channel_id=1, source_target_pairs={{0,4},{2,6},{4,0},{6,2},{8,12},{10,14},{12,8},{14,10},{16,20},{18,... | collective-permute-start | bytes 1544 | tf_op jit(solution)/shard_map/ppermute | solution.py:145
  15.2 1.5 %collective-permute-done.1.swapped_ref = f32[2,64]{1,0:T(2,128)S(1)} collective-permute-done((f32[2,64]{1,0:T(2,128)S(1)}, f32[2,64]{1,0:T(2,128)S(1)}, u32[]{:S(2)}, u32[]{:S(2)}) %collective-permute-start.1) | collective-permute-done | bytes 544 | tf_op jit(solution)/shard_map/ppermute | solution.py:145
  16.8 0.0 copy-start.4
  16.8 0.5 copy-done.4
  17.3 0.0 copy-start
  17.3 0.0 copy-start.1
  17.3 17.1 %all-to-all-start = ((bf16[64,8,512]{2,1,0:T(8,128)(2,1)}), bf16[64,8,512]{2,1,0:T(8,128)(2,1)S(1)}, u32[]{:S(2)}, u32[]{:S(2)}) async-start(bf16[64,8,512]{2,1,0:T(8,128)(2,1)} %after.1), calls=%async_computation | async-start | bytes 1048576 | tf_op jit(solution)/shard_map/all_to_all | solution.py:183
  34.4 0.6 slice_add_fusion
  35.0 0.6 collective-permute-start.2
  35.7 0.0 collective-permute-done.2
  35.7 0.0 copy-start.5
  35.7 0.7 collective-permute-start.3
  36.4 0.0 collective-permute-done.3
  36.4 0.0 copy-done.5
  36.5 1.9 %collective-permute-start.4 = (f32[4,64]{1,0:T(4,128)S(1)}, f32[4,64]{1,0:T(4,128)S(1)}, u32[]{:S(2)}, u32[]{:S(2)}) collective-permute-start(f32[4,64]{1,0:T(4,128)S(1)} %pad_maximum_fusion.1), channel_id=1, source_target_pairs={{0,1},{1,0},{2,3},{3,2},{4,5},{5,4},{6,7},{7,6},{8,9},{9,8},{10,11... | collective-permute-start | bytes 3080 | tf_op jit(solution)/shard_map/ppermute | solution.py:188
  38.4 1.1 %collective-permute-done.4 = f32[4,64]{1,0:T(4,128)S(1)} collective-permute-done((f32[4,64]{1,0:T(4,128)S(1)}, f32[4,64]{1,0:T(4,128)S(1)}, u32[]{:S(2)}, u32[]{:S(2)}) %collective-permute-start.4) | collective-permute-done | bytes 1056 | tf_op jit(solution)/shard_map/ppermute | solution.py:188
  39.5 16.7 %all-to-all-done = bf16[64,8,512]{2,1,0:T(8,128)(2,1)S(1)} async-done(((bf16[64,8,512]{2,1,0:T(8,128)(2,1)}), bf16[64,8,512]{2,1,0:T(8,128)(2,1)S(1)}, u32[]{:S(2)}, u32[]{:S(2)}) %all-to-all-start) | async-done | bytes 524320 | tf_op jit(solution)/shard_map/all_to_all | solution.py:183
  56.2 0.0 copy-done
  56.2 0.0 copy-done.1
  56.2 1.3 %block.1 = bf16[64,9,4,128]{3,2,1,0:T(4,128)(2,1)S(1)} custom-call(bf16[512,512]{1,0:T(8,128)(2,1)S(1)} %bitcast.6, bf16[512,512]{1,0:T(8,128)(2,1)S(1)} %bitcast.7, bf16[512,512]{1,0:T(8,128)(2,1)S(1)} %bitcast.8, f32[8,64]{1,0:T(8,128)S(1)} %pad_maximum_fusion.sums_ref), custom_call_target="tpu_custom_call" | custom-call | tf_op jit(solution)/shard_map/block/pallas_call | solution.py:192
  57.6 0.0 copy-start.2
  57.6 32.7 %all_to_all.10.rows_ref = bf16[64,9,4,128]{3,2,1,0:T(4,128)(2,1)S(1)} all-to-all(bf16[64,9,4,128]{3,2,1,0:T(4,128)(2,1)S(1)} %block.1), channel_id=1, replica_groups=mesh['dp'=64,'mp'=8] {'dp'}, dimensions={0} | all-to-all | bytes 1179648 | tf_op jit(solution)/shard_map/all_to_all | solution.py:201
  90.3 0.0 copy-done.2
  90.3 1.5 %finish.1 = bf16[64,8,512]{2,1,0:T(8,128)(2,1)} custom-call(s32[1,64]{1,0:T(1,128)S(1)} %copy-done.2, bf16[64,9,4,128]{3,2,1,0:T(4,128)(2,1)S(1)} %all_to_all.10.rows_ref), custom_call_target="tpu_custom_call" | custom-call | tf_op jit(solution)/shard_map/finish/pallas_call | solution.py:202
  (7 shorter events, 0.0 us)
Async XLA Ops:
  2.0 0.6 copy-start.3
  2.6 5.4 %collective-permute-start = (f32[1,64]{1,0:T(1,128)S(1)}, f32[1,64]{1,0:T(1,128)S(1)}, u32[]{:S(2)}, u32[]{:S(2)}) collective-permute-start(f32[1,64]{1,0:T(1,128)S(1)} %copy-done.3), channel_id=1, source_target_pairs={{0,2},{2,0},{4,6},{6,4},{8,10},{10,8},{12,14},{14,12},{16,18},{18,... | collective-permute-start | bytes 776 | tf_op jit(solution)/shard_map/ppermute | solution.py:145
  8.0 8.7 %collective-permute-start.1 = (f32[2,64]{1,0:T(2,128)S(1)}, f32[2,64]{1,0:T(2,128)S(1)}, u32[]{:S(2)}, u32[]{:S(2)}) collective-permute-start(f32[2,64]{1,0:T(2,128)S(1)} %pad_maximum_fusion.2), channel_id=1, source_target_pairs={{0,4},{2,6},{4,0},{6,2},{8,12},{10,14},{12,8},{14,10},{16,20},{18,... | collective-permute-start | bytes 1544 | tf_op jit(solution)/shard_map/ppermute | solution.py:145
  16.8 0.5 copy-start.4
  17.3 38.9 %copy-start = (bf16[1,1,512,512]{3,2,1,0:T(8,128)(2,1)S(1)}, bf16[1,1,512,512]{3,2,1,0:T(8,128)(2,1)}, u32[]{:S(2)}) copy-start(bf16[1,1,512,512]{3,2,1,0:T(8,128)(2,1)} %param.6) | copy-start | bytes 1572868
  17.3 38.9 %copy-start.1 = (bf16[1,1,512,512]{3,2,1,0:T(8,128)(2,1)S(1)}, bf16[1,1,512,512]{3,2,1,0:T(8,128)(2,1)}, u32[]{:S(2)}) copy-start(bf16[1,1,512,512]{3,2,1,0:T(8,128)(2,1)} %param.7) | copy-start | bytes 1572868
  17.3 38.9 %all-to-all-start = ((bf16[64,8,512]{2,1,0:T(8,128)(2,1)}), bf16[64,8,512]{2,1,0:T(8,128)(2,1)S(1)}, u32[]{:S(2)}, u32[]{:S(2)}) async-start(bf16[64,8,512]{2,1,0:T(8,128)(2,1)} %after.1), calls=%async_computation | async-start | bytes 1048576 | tf_op jit(solution)/shard_map/all_to_all | solution.py:183
  35.0 0.7 collective-permute-start.2
  35.7 0.7 copy-start.5
  35.7 0.7 collective-permute-start.3
  36.5 3.1 %collective-permute-start.4 = (f32[4,64]{1,0:T(4,128)S(1)}, f32[4,64]{1,0:T(4,128)S(1)}, u32[]{:S(2)}, u32[]{:S(2)}) collective-permute-start(f32[4,64]{1,0:T(4,128)S(1)} %pad_maximum_fusion.1), channel_id=1, source_target_pairs={{0,1},{1,0},{2,3},{3,2},{4,5},{5,4},{6,7},{7,6},{8,9},{9,8},{10,11... | collective-permute-start | bytes 3080 | tf_op jit(solution)/shard_map/ppermute | solution.py:188
  57.6 32.7 %copy-start.2 = (s32[1,64]{1,0:T(1,128)S(1)}, s32[1,64]{1,0:T(1,128)}, u32[]{:S(2)}) copy-start(s32[1,64]{1,0:T(1,128)} %slot_table_ref.1) | copy-start | bytes 772

commit v2 on v1

--- a/solution.py
+++ b/solution.py
@@ -87,6 +87,11 @@
     del rows_ref, swapped_ref, out_ref
 
 
+def again_kernel(partial_ref, rows_ref, out_ref):
+    del rows_ref
+    out_ref[...] = partial_ref[...]
+
+
 def block_kernel(block_ref, left_ref, right_ref, sums_ref, out_ref):
     slots, places = out_ref.shape[0:2]
     order, cols = block_ref.shape
@@ -181,10 +186,17 @@
         name="after",
     )(row_tiles, second)
     blocks = lax.all_to_all(row_tiles, "dp", split_axis=0, concat_axis=0, tiled=True)
-    again = partial + second[0:1]
+    again = pl.pallas_call(
+        again_kernel,
+        out_shape=jax.ShapeDtypeStruct((1, slots), jnp.float32),
+        in_specs=[VMEM, pl.BlockSpec(memory_space=pl.ANY)],
+        out_specs=VMEM,
+        compiler_params=PARAMS,
+        name="again",
+    )(partial, row_tiles)
     first_1 = swapped(again, n_mp, 1, 2)
     second_1 = swapped(jnp.concatenate([again, first_1], axis=0), n_mp, 1, 4)
-    own = jnp.concatenate([partial, first + first_1, second + second_1], axis=0)
+    own = jnp.concatenate([again, first + first_1, second + second_1], axis=0)
     other = lax.ppermute(own, "mp", [(i, i ^ 1) for i in range(n_mp)])
     sums = jnp.concatenate([own, other], axis=0)
 

time: 92.1 us -> 91.7 us (level)
  transfers between devices with their start and end apart: 6 -> 6, of which waited for: 4 -> 4; matrix products, arithmetic and copies ran while one was open for 1% -> 0% of each run, Pallas kernels for 0% -> 0%
where the time goes in v2:
time: 91.7 us; the launch traced here: 91.3 us
  blocking collectives  32.2 us (35%)
  starting transfers between devices  30.4 us (33%)
  waiting for transfers between devices  22.5 us (25%)
  Pallas kernels  4.78 us (5%)
  local copies, waits for them, and re-layouts  1.2 us (1%)
    all_to_all x1, blocking collectives, on_device(): lax.all_to_all(scaled, 'dp', split_axis=0, concat_axis=0, tiled=True)  32.2 us
    all_to_all x1, waiting for transfers between devices, on_device(): lax.all_to_all(row_tiles, 'dp', split_axis=0, concat_axis=0, tiled=True)  17.2 us
    all_to_all x1, starting transfers between devices, on_device(): lax.all_to_all(row_tiles, 'dp', split_axis=0, concat_axis=0, tiled=True)  17.1 us
    ppermute x4, starting transfers between devices, swapped(): lax.ppermute(value, 'mp', [(i, i ^ step) for i in range(core, size, 2)])  11.4 us
    ppermute x4, waiting for transfers between devices, swapped(): lax.ppermute(value, 'mp', [(i, i ^ step) for i in range(core, size, 2)])  4.23 us
    pallas_call x1, Pallas kernels, on_device(): pl.pallas_call(send_kernel, out_shape=(jax.ShapeDtypeStruct((slots, rows,...  1.98 us
    ppermute x1, starting transfers between devices, on_device(): other = lax.ppermute(own, 'mp', [(i, i ^ 1) for i in range(n_mp)])  1.92 us
  transfers between devices with their start and end apart: 6, of which 4 were waited for; matrix products, arithmetic and copies ran while one was open for 0% of the time, Pallas kernels for 0%

profile of v2, /device:TPU:6, one launch (start us, length us, event | category | flops | bytes accessed | tf_op | source)
XLA Modules:
  0.0 91.3 jit_solution(381312237113842596)
XLA Ops:
  0.0 2.0 %send.1 = (bf16[64,8,512]{2,1,0:T(8,128)(2,1)}, f32[1,64]{1,0:T(1,128)}) custom-call(s32[1,64]{1,0:T(1,128)} %slot_table_ref.1, s32[1,64]{1,0:T(1,128)} %bitcast.10, bf16[64,8,512]{2,1,0:T(8,128)(2,1)} %bitcast.9), custom_call_target="tpu_custom_call" | custom-call | tf_op jit(solution)/shard_map/send/pallas_call | solution.py:157
  2.0 0.0 copy-start.4
  2.0 0.6 copy-done.4
  2.6 2.7 %collective-permute-start = (f32[1,64]{1,0:T(1,128)S(1)}, f32[1,64]{1,0:T(1,128)S(1)}, u32[]{:S(2)}, u32[]{:S(2)}) collective-permute-start(f32[1,64]{1,0:T(1,128)S(1)} %copy-done.4), channel_id=1, source_target_pairs={{0,2},{2,0},{4,6},{6,4},{8,10},{10,8},{12,14},{14,12},{16,18},{18,... | collective-permute-start | bytes 776 | tf_op jit(solution)/shard_map/ppermute | solution.py:150
  5.4 2.7 %collective-permute-done = f32[1,64]{1,0:T(1,128)S(1)} collective-permute-done((f32[1,64]{1,0:T(1,128)S(1)}, f32[1,64]{1,0:T(1,128)S(1)}, u32[]{:S(2)}, u32[]{:S(2)}) %collective-permute-start) | collective-permute-done | bytes 288 | tf_op jit(solution)/shard_map/ppermute | solution.py:150
  8.1 7.2 %collective-permute-start.1 = (f32[2,64]{1,0:T(2,128)S(1)}, f32[2,64]{1,0:T(2,128)S(1)}, u32[]{:S(2)}, u32[]{:S(2)}) collective-permute-start(f32[2,64]{1,0:T(2,128)S(1)} %pad_maximum_fusion.2), channel_id=1, source_target_pairs={{0,4},{2,6},{4,0},{6,2},{8,12},{10,14},{12,8},{14,10},{16,20},{18,... | collective-permute-start | bytes 1544 | tf_op jit(solution)/shard_map/ppermute | solution.py:150
  15.3 1.5 %collective-permute-done.1.swapped_ref = f32[2,64]{1,0:T(2,128)S(1)} collective-permute-done((f32[2,64]{1,0:T(2,128)S(1)}, f32[2,64]{1,0:T(2,128)S(1)}, u32[]{:S(2)}, u32[]{:S(2)}) %collective-permute-start.1) | collective-permute-done | bytes 544 | tf_op jit(solution)/shard_map/ppermute | solution.py:150
  16.8 0.0 copy-start.5
  16.8 0.5 copy-done.5
  17.4 0.0 copy-start
  17.4 0.0 copy-start.2
  17.4 17.1 %all-to-all-start = ((bf16[64,8,512]{2,1,0:T(8,128)(2,1)}), bf16[64,8,512]{2,1,0:T(8,128)(2,1)S(1)}, u32[]{:S(2)}, u32[]{:S(2)}) async-start(bf16[64,8,512]{2,1,0:T(8,128)(2,1)} %after.1.rows_ref), calls=%async_computation | async-start | bytes 1048576 | tf_op jit(solution)/shard_map/all_to_all | solution.py:188
  34.4 0.0 copy-done
  34.5 0.0 copy-start.1
  34.5 0.8 collective-permute-start.2
  35.3 0.0 collective-permute-done.2
  35.3 0.0 copy-start.6
  35.3 0.7 collective-permute-start.3
  36.0 0.0 collective-permute-done.3
  36.0 0.0 copy-done.6
  36.0 1.9 %collective-permute-start.4 = (f32[4,64]{1,0:T(4,128)S(1)}, f32[4,64]{1,0:T(4,128)S(1)}, u32[]{:S(2)}, u32[]{:S(2)}) collective-permute-start(f32[4,64]{1,0:T(4,128)S(1)} %pad_maximum_fusion.1), channel_id=1, source_target_pairs={{0,1},{1,0},{2,3},{3,2},{4,5},{5,4},{6,7},{7,6},{8,9},{9,8},{10,11... | collective-permute-start | bytes 3080 | tf_op jit(solution)/shard_map/ppermute | solution.py:200
  38.0 1.1 %collective-permute-done.4 = f32[4,64]{1,0:T(4,128)S(1)} collective-permute-done((f32[4,64]{1,0:T(4,128)S(1)}, f32[4,64]{1,0:T(4,128)S(1)}, u32[]{:S(2)}, u32[]{:S(2)}) %collective-permute-start.4) | collective-permute-done | bytes 1056 | tf_op jit(solution)/shard_map/ppermute | solution.py:200
  39.1 17.2 %all-to-all-done = bf16[64,8,512]{2,1,0:T(8,128)(2,1)S(1)} async-done(((bf16[64,8,512]{2,1,0:T(8,128)(2,1)}), bf16[64,8,512]{2,1,0:T(8,128)(2,1)S(1)}, u32[]{:S(2)}, u32[]{:S(2)}) %all-to-all-start) | async-done | bytes 524320 | tf_op jit(solution)/shard_map/all_to_all | solution.py:188
  56.3 0.0 copy-done.2
  56.3 0.0 copy-done.1
  56.3 1.3 %block.1 = bf16[64,9,4,128]{3,2,1,0:T(4,128)(2,1)S(1)} custom-call(bf16[512,512]{1,0:T(8,128)(2,1)S(1)} %bitcast.6, bf16[512,512]{1,0:T(8,128)(2,1)S(1)} %bitcast.7, bf16[512,512]{1,0:T(8,128)(2,1)S(1)} %bitcast.8, f32[8,64]{1,0:T(8,128)S(1)} %pad_maximum_fusion.sums_ref), custom_call_target="tpu_custom_call" | custom-call | tf_op jit(solution)/shard_map/block/pallas_call | solution.py:204
  57.6 0.0 copy-start.3
  57.6 32.2 %all_to_all.10.rows_ref = bf16[64,9,4,128]{3,2,1,0:T(4,128)(2,1)S(1)} all-to-all(bf16[64,9,4,128]{3,2,1,0:T(4,128)(2,1)S(1)} %block.1), channel_id=1, replica_groups=mesh['dp'=64,'mp'=8] {'dp'}, dimensions={0} | all-to-all | bytes 1179648 | tf_op jit(solution)/shard_map/all_to_all | solution.py:213
  89.8 0.0 copy-done.3
  89.8 1.5 %finish.1 = bf16[64,8,512]{2,1,0:T(8,128)(2,1)} custom-call(s32[1,64]{1,0:T(1,128)S(1)} %copy-done.3, bf16[64,9,4,128]{3,2,1,0:T(4,128)(2,1)S(1)} %all_to_all.10.rows_ref), custom_call_target="tpu_custom_call" | custom-call | tf_op jit(solution)/shard_map/finish/pallas_call | solution.py:214
  (8 shorter events, 0.1 us)
Async XLA Ops:
  2.0 0.6 copy-start.4
  2.6 5.4 %collective-permute-start = (f32[1,64]{1,0:T(1,128)S(1)}, f32[1,64]{1,0:T(1,128)S(1)}, u32[]{:S(2)}, u32[]{:S(2)}) collective-permute-start(f32[1,64]{1,0:T(1,128)S(1)} %copy-done.4), channel_id=1, source_target_pairs={{0,2},{2,0},{4,6},{6,4},{8,10},{10,8},{12,14},{14,12},{16,18},{18,... | collective-permute-start | bytes 776 | tf_op jit(solution)/shard_map/ppermute | solution.py:150
  8.1 8.7 %collective-permute-start.1 = (f32[2,64]{1,0:T(2,128)S(1)}, f32[2,64]{1,0:T(2,128)S(1)}, u32[]{:S(2)}, u32[]{:S(2)}) collective-permute-start(f32[2,64]{1,0:T(2,128)S(1)} %pad_maximum_fusion.2), channel_id=1, source_target_pairs={{0,4},{2,6},{4,0},{6,2},{8,12},{10,14},{12,8},{14,10},{16,20},{18,... | collective-permute-start | bytes 1544 | tf_op jit(solution)/shard_map/ppermute | solution.py:150
  16.8 0.5 copy-start.5
  17.4 17.1 %copy-start = (bf16[64,8,512]{2,1,0:T(8,128)(2,1)S(1)}, bf16[64,8,512]{2,1,0:T(8,128)(2,1)}, u32[]{:S(2)}) copy-start(bf16[64,8,512]{2,1,0:T(8,128)(2,1)} %after.1.rows_ref) | copy-start | bytes 1572868
  17.4 38.9 %copy-start.2 = (bf16[1,1,512,512]{3,2,1,0:T(8,128)(2,1)S(1)}, bf16[1,1,512,512]{3,2,1,0:T(8,128)(2,1)}, u32[]{:S(2)}) copy-start(bf16[1,1,512,512]{3,2,1,0:T(8,128)(2,1)} %param.7) | copy-start | bytes 1572868
  17.4 38.9 %all-to-all-start = ((bf16[64,8,512]{2,1,0:T(8,128)(2,1)}), bf16[64,8,512]{2,1,0:T(8,128)(2,1)S(1)}, u32[]{:S(2)}, u32[]{:S(2)}) async-start(bf16[64,8,512]{2,1,0:T(8,128)(2,1)} %after.1.rows_ref), calls=%async_computation | async-start | bytes 1048576 | tf_op jit(solution)/shard_map/all_to_all | solution.py:188
  34.5 21.8 %copy-start.1 = (bf16[1,1,512,512]{3,2,1,0:T(8,128)(2,1)S(1)}, bf16[1,1,512,512]{3,2,1,0:T(8,128)(2,1)}, u32[]{:S(2)}) copy-start(bf16[1,1,512,512]{3,2,1,0:T(8,128)(2,1)} %param.6) | copy-start | bytes 1572868
  34.5 0.8 collective-permute-start.2
  35.3 0.7 copy-start.6
  35.3 0.7 collective-permute-start.3
  36.0 3.1 %collective-permute-start.4 = (f32[4,64]{1,0:T(4,128)S(1)}, f32[4,64]{1,0:T(4,128)S(1)}, u32[]{:S(2)}, u32[]{:S(2)}) collective-permute-start(f32[4,64]{1,0:T(4,128)S(1)} %pad_maximum_fusion.1), channel_id=1, source_target_pairs={{0,1},{1,0},{2,3},{3,2},{4,5},{5,4},{6,7},{7,6},{8,9},{9,8},{10,11... | collective-permute-start | bytes 3080 | tf_op jit(solution)/shard_map/ppermute | solution.py:200
  57.6 32.2 %copy-start.3 = (s32[1,64]{1,0:T(1,128)S(1)}, s32[1,64]{1,0:T(1,128)}, u32[]{:S(2)}) copy-start(s32[1,64]{1,0:T(1,128)} %slot_table_ref.1) | copy-start | bytes 772
